TPU v7x, 256 devices: a whole 4x4x8 slice. The times are simulated.
256 devices in a mesh: src: 8 (over x_hi, y), dst: 32 (over z, x_lo, core).
Axes of the slice: x: 4 (x_hi: 2, x_lo: 2; x = x_hi * 2 + x_lo), y: 4, z: 8, core: 2. Of those that a mesh axis runs over, the one named last changes fastest.
Arguments:
- src_rows: float32 [131072, 200], P(('src', 'dst')), may hold values from -10 to 10
- src_state: float32 [131072], P(('src', 'dst')), may hold values from 0.02 to 2
- dst_rows: float32 [131072, 200], P(('src', 'dst')), may hold values from -10 to 10
- dst_state: float32 [131072], P(('src', 'dst')), may hold values from 0.02 to 2
- relations: float32 [1024, 200], replicated, may hold values from 0.1 to 1.9
- relation_state: float32 [1024], replicated, may hold values from 1 to 100
- block_tiles: int32 [2, 4096, 2], P(None, ('src', 'dst')), may hold values from 0 to 3
- src_offsets: int32 [2, 4096, 128], P(None, ('src', 'dst')), may hold values from 0 to 127
- dst_offsets: int32 [2, 4096, 128], P(None, ('src', 'dst')), may hold values from 0 to 127
- relation_ids: int32 [2, 4096, 128], P(None, ('src', 'dst')), may hold values from 0 to 1023
- negative_ids: int32 [2, 4096, 50], P(None, ('src', 'dst')), may hold values from 0 to 511
Outputs:
- src_out: float32 [131072, 200], P(('src', 'dst'))
- dst_out: float32 [131072, 200], P(('src', 'dst'))
- rel_out: float32 [1024, 200], replicated
Inputs may be any that keep to these rules, and one draw needn't show every extreme that they name: `block_tiles`: entry 0 names the block's tile of 128 source rows, entry 1 its tile of 128 slab rows, both within the partition; all edges of a block lie in these two tiles. `negative_ids`: rows within the slab held in that round.
All inputs are finite; a program needn't handle non-finite values.
Results may differ from a plain program's by a relative error of at most 0.0001.
Values sent between devices are 32-bit elements; how exact they have to be, the bound alone decides.
A program may use at most 64 MiB of HBM per device.

v0:
```python
import jax
import jax.numpy as jnp
from jax import lax
from jax.sharding import PartitionSpec as P

learn_rate = 0.1
highest = lax.Precision.HIGHEST


def passed_along(value, axis, by):
    size = lax.axis_size(axis)
    return lax.ppermute(value, axis, [(i, (i + by) % size) for i in range(size)])


def adagrad(entries, squares, gradient):
    new_squares = squares + jnp.mean(gradient * gradient, axis=-1)
    return (entries - learn_rate * gradient / jnp.sqrt(new_squares)[:, None], new_squares)


def tile_selector(tile_ids, tile_count):
    return (tile_ids[:, None] == jnp.arange(tile_count, dtype=jnp.int32)[None, :]).astype(
        jnp.float32
    )


def fetch_tiles(entries, selector, tile_rows):
    features = entries.shape[1]
    flattened = entries.reshape(selector.shape[1], tile_rows * features)
    picked = jnp.dot(selector, flattened, precision=highest, preferred_element_type=jnp.float32)
    return picked.reshape(selector.shape[0], tile_rows, features)


def store_tiles(pieces, selector):
    block_count, tile_rows, features = pieces.shape
    flattened = pieces.reshape(block_count, tile_rows * features)
    summed = jnp.dot(selector.T, flattened, precision=highest, preferred_element_type=jnp.float32)
    return summed.reshape(selector.shape[1] * tile_rows, features)


def row_selector(offsets, tile_rows):
    return (offsets[:, :, None] == jnp.arange(tile_rows, dtype=jnp.int32)[None, None, :]).astype(
        jnp.float32
    )


def local_terms(sources, slab, rel_table, tile_ids, src_off, dst_off, rel_ids, neg_ids):
    tile_rows = src_off.shape[1]
    tile_count = sources.shape[0] // tile_rows
    features = sources.shape[1]
    neg_count = neg_ids.shape[1]
    src_pick = tile_selector(tile_ids[:, 0], tile_count)
    dst_pick = tile_selector(tile_ids[:, 1], tile_count)
    src_tiles = fetch_tiles(sources, src_pick, tile_rows)
    dst_tiles = fetch_tiles(slab, dst_pick, tile_rows)
    src_select = row_selector(src_off, tile_rows)
    dst_select = row_selector(dst_off, tile_rows)
    head_rows = jnp.einsum("ber,brd->bed", src_select, src_tiles, precision=highest)
    tail_rows = jnp.einsum("ber,brd->bed", dst_select, dst_tiles, precision=highest)
    diagonal = jnp.take(rel_table, rel_ids, axis=0)
    neg_rows = jnp.take(slab, neg_ids, axis=0)
    lifted = head_rows * diagonal
    positive = jnp.sum(lifted * tail_rows, axis=-1)
    negative = jnp.einsum("bed,bnd->ben", lifted, neg_rows, precision=highest)
    pos_weight = -jax.nn.sigmoid(-positive)
    neg_weight = jax.nn.sigmoid(negative) / neg_count
    pulled = pos_weight[..., None] * tail_rows + jnp.einsum(
        "ben,bnd->bed", neg_weight, neg_rows, precision=highest
    )
    head_grad = pulled * diagonal
    diag_grad = pulled * head_rows
    tail_grad = pos_weight[..., None] * lifted
    neg_grad = jnp.einsum("ben,bed->bnd", neg_weight, lifted, precision=highest)
    src_grad = store_tiles(
        jnp.einsum("ber,bed->brd", src_select, head_grad, precision=highest), src_pick
    )
    slab_grad = store_tiles(
        jnp.einsum("ber,bed->brd", dst_select, tail_grad, precision=highest), dst_pick
    )
    slab_grad = slab_grad.at[neg_ids.reshape(-1)].add(neg_grad.reshape(-1, features))
    rel_grad = (
        jnp.zeros(rel_table.shape, jnp.float32)
        .at[rel_ids.reshape(-1)]
        .add(diag_grad.reshape(-1, features))
    )
    return (src_grad, slab_grad, rel_grad)


def shards(
    src_rows,
    src_state,
    dst_rows,
    dst_state,
    relations,
    relation_state,
    block_tiles,
    src_offsets,
    dst_offsets,
    relation_ids,
    negative_ids,
):
    sources = src_rows
    source_sq = src_state
    slab = dst_rows
    slab_sq = dst_state
    rel_table = relations
    rel_sq = relation_state
    for round_index in range(block_tiles.shape[0]):
        src_grad, slab_grad, rel_local = local_terms(
            sources,
            slab,
            rel_table,
            block_tiles[round_index],
            src_offsets[round_index],
            dst_offsets[round_index],
            relation_ids[round_index],
            negative_ids[round_index],
        )
        rel_grad = lax.psum(rel_local, ("src", "dst"))
        sources, source_sq = adagrad(sources, source_sq, src_grad)
        rel_table, rel_sq = adagrad(rel_table, rel_sq, rel_grad)
        slab, slab_sq = adagrad(slab, slab_sq, slab_grad)
        slab, slab_sq = passed_along((slab, slab_sq), "dst", 1)
    return (sources, slab, rel_table)


def solution(mesh):
    return jax.shard_map(
        shards,
        mesh=mesh,
        in_specs=(
            P(("src", "dst"), None),
            P(("src", "dst")),
            P(("src", "dst"), None),
            P(("src", "dst")),
            P(),
            P(),
            P(None, ("src", "dst"), None),
            P(None, ("src", "dst"), None),
            P(None, ("src", "dst"), None),
            P(None, ("src", "dst"), None),
            P(None, ("src", "dst"), None),
        ),
        out_specs=(P(("src", "dst"), None), P(("src", "dst"), None), P()),
        check_vma=False,
    )
```

profile of v0, /device:TPU:1, one launch (start us, length us, event | category | flops | bytes accessed | tf_op | source)
XLA Modules:
  0.0 676.1 jit_solution(3683382634482203033)
XLA Ops:
  18.1 7.6 %gather_fusion = f32[2048,200]{1,0:T(8,128)S(1)} fusion(f32[1024,200]{1,0:T(8,128)S(1)} %copy.23, s32[2048]{0:T(1024)} %get-tuple-element.32), kind=kCustom, calls=%fused_computation.clone | custom fusion | bytes 3284992 | tf_op jit(solution)/shard_map/jit(_take)/gather | solution.py:59
  30.9 2.7 gather_fusion.1
  39.7 2.2 multiply_reduce_fusion.1
  44.2 4.8 fusion.101
  49.0 2.8 copy.58
  51.8 13.2 %scatter_custom_fusion = f32[1024,200]{1,0:T(8,128)} fusion(s32[2048]{0:T(1024)S(1)} %bitcast.103, f32[2048,200]{1,0:T(8,128)} %bitcast.95, f32[]{:T(128)} %constant.25.clone.1), kind=kCustom, calls=%fused_computation.73 | custom fusion | flops 409600 | bytes 819712 | tf_op jit(solution)/shard_map/scatter-add | solution.py:83
  65.1 3.3 fusion.12
  68.4 4.2 fusion.103
  72.6 3.1 reshape.213
  80.4 6.3 scatter_fusion
  88.4 3.0 collective-permute-start
  91.5 5.0 fusion.14
  96.5 3.1 reshape.210
  101.2 2.7 mul.106
  111.5 3.1 fusion.2
  115.3 208.2 %all-reduce.3.cloned.1.call-done = f32[1024,200]{1,0:T(8,128)} async-done(((f32[1024,200]{1,0:T(8,128)}), f32[1024,200]{1,0:T(8,128)}) %all-reduce.3.cloned.1.call-update) | async-done | bytes 819216 | tf_op jit(solution)/shard_map/psum | solution.py:118
  326.3 8.6 %gather_fusion.2 = f32[2048,200]{1,0:T(8,128)} fusion(f32[1024,200]{1,0:T(8,128)S(1)} %divide_subtract_fusion.1, s32[2048]{0:T(1024)S(1)} %copy-done.23), kind=kCustom, calls=%fused_computation.2.clone | custom fusion | bytes 3284992 | tf_op jit(solution)/shard_map/jit(_take)/gather | solution.py:59
  334.9 2.8 copy.34
  339.3 3.4 gather_fusion.3
  345.3 3.4 multiply_reduce_fusion
  348.7 3.5 fusion.8
  354.3 4.3 fusion.104
  358.6 4.3 fusion.102
  362.9 3.4 fusion.10
  366.3 4.2 reshape.217
  370.5 2.2 broadcast_multiply_fusion
  375.8 4.2 reshape.218
  386.1 6.8 %scatter_fusion.1 = f32[512,200]{1,0:T(8,128)S(1)} fusion(f32[512,200]{1,0:T(8,128)S(1)} %reshape.219, s32[800]{0:T(1024)S(1)} %copy-done.33, f32[800,200]{1,0:T(8,128)} %reshape.274), kind=kCustom, calls=%fused_computation.6 | custom fusion | flops 160000 | bytes 1923200 | tf_op jit(solution)/shard_map/scatter-add | solution.py:79
  394.0 3.1 copy.61
  397.1 13.0 %scatter_custom_fusion.3 = f32[1024,200]{1,0:T(8,128)} fusion(s32[2048]{0:T(1024)} %bitcast.102, f32[2048,200]{1,0:T(8,128)} %bitcast.94, f32[]{:T(128)} %constant.25.clone.1), kind=kCustom, calls=%fused_computation.71 | custom fusion | flops 409600 | bytes 819712 | tf_op jit(solution)/shard_map/scatter-add | solution.py:83
  410.9 3.4 collective-permute-start.2
  414.3 250.5 %all-reduce.5.cloned.1.call-done = f32[1024,200]{1,0:T(8,128)} async-done(((f32[1024,200]{1,0:T(8,128)}), f32[1024,200]{1,0:T(8,128)}) %all-reduce.5.cloned.1.call-update) | async-done | bytes 819216 | tf_op jit(solution)/shard_map/psum | solution.py:118
  (190 shorter events, 64.5 us)
Async XLA Ops:
  7.2 316.3 %all-reduce.3.cloned.1.call-start = ((), (), s32[]{:S(2)}) async-start(), calls=%async_computation | async-start | bytes 2097152 | tf_op jit(solution)/shard_map/psum | solution.py:118
  13.8 2.8 copy-start.50
  13.8 3.4 copy-start.34
  27.5 2.8 copy-start.35
  35.3 3.0 copy-start.46
  35.3 3.0 copy-start.42
  44.2 4.8 copy-start.9
  65.0 3.4 copy-start.13
  65.0 599.8 %all-reduce.5.cloned.1.call-start = ((), (), s32[]{:S(2)}) async-start(), calls=%async_computation.1 | async-start | bytes 2097152 | tf_op jit(solution)/shard_map/psum | solution.py:118
  65.1 3.3 copy-start.10
  72.6 3.1 copy-start.43
  80.4 6.5 copy-start.51
  86.7 4.8 copy-start.2
  86.7 4.7 copy-start.18
  88.4 249.3 %collective-permute-start = (f32[512,200]{1,0:T(8,128)}, f32[512,200]{1,0:T(8,128)S(1)}, u32[]{:S(2)}, u32[]{:S(2)}) collective-permute-start(f32[512,200]{1,0:T(8,128)} %divide_subtract_fusion.4), channel_id=1, source_target_pairs={{0,1},{1,2},{2,3},{3,4},{4,5},{5,6},{6,7},{7,8},{8,9},{9,10},{10,1... | collective-permute-start | bytes 1228808 | tf_op jit(solution)/shard_map/ppermute | solution.py:12
  91.4 318.7 %collective-permute-start.1 = (f32[512]{0:T(512)}, f32[512]{0:T(512)}, u32[]{:S(2)}, u32[]{:S(2)}) collective-permute-start(f32[512]{0:T(512)} %get-tuple-element.14), channel_id=1, source_target_pairs={{0,1},{1,2},{2,3},{3,4},{4,5},{5,6},{6,7},{7,8},{8,9},{9,10},{10,1... | collective-permute-start | bytes 6152 | tf_op jit(solution)/shard_map/ppermute | solution.py:12
  96.5 3.1 copy-start.47
  101.2 5.2 copy-start.39
  101.2 5.2 copy-start.6
  107.7 3.0 copy-start.44
  111.5 3.2 copy-start.24
  111.5 214.1 %copy-start.36 = (f32[1024]{0:T(1024)S(1)}, f32[1024]{0:T(1024)}, u32[]{:S(2)}) copy-start(f32[1024]{0:T(1024)} %param.20) | copy-start | bytes 12292
  348.7 3.5 copy-start.30
  358.6 4.3 copy-start.3
  358.6 4.3 copy-start.15
  366.3 4.2 copy-start.45
  375.8 4.2 copy-start.41
  382.9 3.1 copy-start.33
  386.1 6.9 %copy-start.11 = (f32[512,200]{1,0:T(8,128)S(1)}, f32[512,200]{1,0:T(8,128)}, u32[]{:S(2)}) copy-start(f32[512,200]{1,0:T(8,128)} %divide_subtract_fusion.3) | copy-start | bytes 1228804
  410.1 256.3 %copy-start.22 = (f32[1024]{0:T(1024)S(1)}, f32[1024]{0:T(1024)}, u32[]{:S(2)}) copy-start(f32[1024]{0:T(1024)} %copy-done.21) | copy-start | bytes 12292
  410.1 256.3 %copy-start.37 = (f32[1024]{0:T(1024)S(1)}, f32[1024]{0:T(1024)}, u32[]{:S(2)}) copy-start(f32[1024]{0:T(1024)} %param.20) | copy-start | bytes 12292
  410.9 256.9 %collective-permute-start.2 = (f32[512,200]{1,0:T(8,128)S(1)}, f32[512,200]{1,0:T(8,128)S(1)}, u32[]{:S(2)}, u32[]{:S(2)}) collective-permute-start(f32[512,200]{1,0:T(8,128)S(1)} %divide_subtract_fusion.2), channel_id=1, source_target_pairs={{0,1},{1,2},{2,3},{3,4},{4,5},{5,6},{6,7},{7,8},{8,9},{9,10},{10,1... | collective-permute-start | bytes 1228808 | tf_op jit(solution)/shard_map/ppermute | solution.py:12
  (25 other events, 43.4 us)
Sparse Core Ops, SparseCore 0:
  65.1 258.3 all-reduce.2
  410.2 254.5 all-reduce.4
where the time goes:
time: 687 us; the launch traced here: 676 us
  waiting for transfers between devices  459 us (67%)
  local copies, waits for them, and re-layouts  80.5 us (12%)
  matrix products  58.8 us (9%)
  other arithmetic  56.2 us (8%)
  between operations  15.4 us (2%)
    psum x2, waiting for transfers between devices, shards(): rel_grad = lax.psum(rel_local, ('src', 'dst'))  459 us
    scatter-add x2, other arithmetic, local_terms(): rel_grad = jnp.zeros(rel_table.shape, jnp.float32).at[rel_ids.reshape(-1)...  26.1 us
    gather x4, local copies, waits for them, and re-layouts, local_terms(): diagonal = jnp.take(rel_table, rel_ids, axis=0)  20.8 us
    reshape x4, local copies, waits for them, and re-layouts, store_tiles(): flattened = pieces.reshape(block_count, tile_rows * features)  14.6 us
  transfers between devices with their start and end apart: 5, of which 2 were waited for; matrix products, arithmetic and copies ran while one was open for 20% of the time, Pallas kernels for 0%

commit v1 on v0

v1 whole, which is shorter than its diff:
```python
import functools

import jax
import jax.numpy as jnp
from jax import lax
from jax.experimental import pallas as pl
from jax.experimental.pallas import tpu as pltpu
from jax.sharding import PartitionSpec as P

MESH = pl.DeviceIdType.MESH
f32, bf16, i32 = jnp.float32, jnp.bfloat16, jnp.int32
learn_rate = 0.1
D, REL, TILE, NEG, ROWS, BLK, ROUNDS = 200, 1024, 128, 50, 512, 16, 2
HALF = REL // 2
EDGES = BLK * TILE
NEGS = BLK * 64
VMEM_LIMIT = 56 << 20


def two_parts(value):
    high = value.astype(bf16)
    return high, (value - high.astype(f32)).astype(bf16)


def stacked(value):
    return jnp.concatenate(two_parts(value), axis=0)


def folded(value):
    half = value.shape[0] // 2
    return value[:half] + value[half:]


def dot(a, b, dims=((1,), (0,))):
    return lax.dot_general(a, b, (dims, ((), ())), preferred_element_type=f32)


NT = ((1,), (1,))
TN = ((0,), (0,))


def lane_pick(tile, offsets):
    index = jnp.broadcast_to(offsets, tile.shape)
    return jnp.take_along_axis(tile, index, axis=1, mode="promise_in_bounds")


def one_hot(ids, rows):
    places = lax.broadcasted_iota(i32, (rows, ids.shape[1]), 0)
    return jnp.where(places == ids, 1.0, 0.0).astype(bf16)


def adagrad(table, sums, grad):
    sums = sums + jnp.sum(grad * grad, axis=0, keepdims=True) * (1.0 / D)
    return table - grad * (learn_rate / jnp.sqrt(sums)), sums


def round_kernel(
    rnd,
    tiles_ref,
    src_ref,
    src_sq_ref,
    slab_ref,
    slab_sq_ref,
    rel_ref,
    src_off_ref,
    dst_off_ref,
    rel_ids_ref,
    neg_ids_ref,
    new_src_ref,
    new_src_sq_ref,
    new_slab_ref,
    new_slab_sq_ref,
    rel_grad_ref,
    rel_parts,
    rel_hot,
    src_hot,
    slab_hot,
    negs,
    src_terms,
    slab_terms,
    rel_terms,
):
    rel_parts[...] = stacked(rel_ref[...])
    slab_parts = stacked(slab_ref[...])
    for p in range(4):
        lanes = pl.ds(p * 256, 256)
        ids = jnp.concatenate(
            [neg_ids_ref[rnd, 2 * p : 2 * p + 1, :], neg_ids_ref[rnd, 2 * p + 1 : 2 * p + 2, :]], axis=1
        )
        hot = one_hot(ids, ROWS)
        slab_hot[:, pl.ds(EDGES + p * 256, 256)] = hot
        negs[:, lanes] = folded(dot(slab_parts, hot))

    def pair(p, carry):
        heads, tails, hots = [], [], []
        for j in range(2):
            b = 2 * p + j
            src_tile = tiles_ref[(rnd * BLK + b) * 2]
            dst_tile = tiles_ref[(rnd * BLK + b) * 2 + 1]
            src_off = src_off_ref[rnd, pl.ds(b, 1), :]
            dst_off = dst_off_ref[rnd, pl.ds(b, 1), :]
            heads.append(lane_pick(src_ref[:, pl.ds(pl.multiple_of(src_tile * TILE, TILE), TILE)], src_off))
            tails.append(lane_pick(slab_ref[:, pl.ds(pl.multiple_of(dst_tile * TILE, TILE), TILE)], dst_off))
            own = pl.ds(pl.multiple_of(b * TILE, TILE), TILE)
            src_hot[:, own] = one_hot(src_off + src_tile * TILE, ROWS)
            slab_hot[:, own] = one_hot(dst_off + dst_tile * TILE, ROWS)
            hots.append(one_hot(rel_ids_ref[rnd, pl.ds(b, 1), :], REL))
        head = jnp.concatenate(heads, axis=1)
        tail = jnp.concatenate(tails, axis=1)
        hot = jnp.concatenate(hots, axis=1)
        both = pl.ds(pl.multiple_of(p * 256, 256), 256)
        rel_hot[:, both] = hot
        diagonal = folded(dot(rel_parts[...], hot))
        lifted = head * diagonal
        lifted_high, lifted_low = two_parts(lifted)
        own_negs = negs[:, pl.ds(pl.multiple_of(p * 128, 128), 128)]
        neg_high, neg_low = two_parts(own_negs)
        positive = jnp.sum(lifted * tail, axis=0, keepdims=True)
        score = (
            dot(neg_high, lifted_high, TN) + dot(neg_low, lifted_high, TN) + dot(neg_high, lifted_low, TN)
        )
        pos_weight = -jax.nn.sigmoid(-positive)
        first = jax.nn.sigmoid(score[:64, :128]) * (1.0 / NEG)
        second = jax.nn.sigmoid(score[64:, 128:]) * (1.0 / NEG)
        nothing = jnp.zeros((64, 128), f32)
        weight = jnp.concatenate(
            [jnp.concatenate([first, nothing], axis=1), jnp.concatenate([nothing, second], axis=1)], axis=0
        )
        weight_high, weight_low = two_parts(weight)
        pulled = (
            pos_weight * tail
            + folded(dot(jnp.concatenate([neg_high, neg_low], axis=0), weight_high))
            + dot(neg_high, weight_low)
        )
        neg_grad = folded(dot(jnp.concatenate([lifted_high, lifted_low], axis=0), weight_high, NT)) + dot(
            lifted_high, weight_low, NT
        )
        src_terms[:, both] = stacked(pulled * diagonal)
        rel_terms[:, both] = stacked(pulled * head)
        slab_terms[:, both] = stacked(pos_weight * lifted)
        slab_terms[:, pl.ds(pl.multiple_of(EDGES + p * 128, 128), 128)] = stacked(neg_grad)
        return carry

    lax.fori_loop(0, BLK // 2, pair, 0)

    def rel_chunk(q, carry):
        rows = pl.ds(pl.multiple_of(q * 256, 256), 256)
        rel_grad_ref[:, rows] = folded(dot(rel_terms[...], rel_hot[rows, :], NT))
        return carry

    lax.fori_loop(0, REL // 256, rel_chunk, 0)

    def row_chunk(q, carry):
        rows = pl.ds(pl.multiple_of(q * 256, 256), 256)
        grad = folded(dot(src_terms[...], src_hot[rows, :], NT))
        new_src_ref[:, rows], new_src_sq_ref[:, rows] = adagrad(src_ref[:, rows], src_sq_ref[:, rows], grad)
        grad = folded(dot(slab_terms[...], slab_hot[rows, :], NT))
        new_slab_ref[:, rows], new_slab_sq_ref[:, rows] = adagrad(slab_ref[:, rows], slab_sq_ref[:, rows], grad)
        return carry

    lax.fori_loop(0, ROWS // 256, row_chunk, 0)


def run_round(rnd, tiles, src, src_sq, slab, slab_sq, rel, src_off, dst_off, rel_ids, neg_ids):
    vmem = pl.BlockSpec(memory_space=pltpu.VMEM)
    return pl.pallas_call(
        functools.partial(round_kernel, rnd),
        out_shape=[
            jax.ShapeDtypeStruct((D, ROWS), f32),
            jax.ShapeDtypeStruct((1, ROWS), f32),
            jax.ShapeDtypeStruct((D, ROWS), f32),
            jax.ShapeDtypeStruct((1, ROWS), f32),
            jax.ShapeDtypeStruct((D, REL), f32),
        ],
        in_specs=[pl.BlockSpec(memory_space=pltpu.SMEM)] + [vmem] * 9,
        out_specs=[vmem] * 5,
        scratch_shapes=[
            pltpu.VMEM((2 * D, REL), bf16),
            pltpu.VMEM((REL, EDGES), bf16),
            pltpu.VMEM((ROWS, EDGES), bf16),
            pltpu.VMEM((ROWS, EDGES + NEGS), bf16),
            pltpu.VMEM((D, NEGS), f32),
            pltpu.VMEM((2 * D, EDGES), bf16),
            pltpu.VMEM((2 * D, EDGES + NEGS), bf16),
            pltpu.VMEM((2 * D, EDGES), bf16),
        ],
        compiler_params=pltpu.CompilerParams(vmem_limit_bytes=VMEM_LIMIT),
        name=f"round{rnd}",
    )(tiles, src, src_sq, slab, slab_sq, rel, src_off, dst_off, rel_ids, neg_ids)


def exchange_kernel(
    grad_ref,
    rel_ref,
    rel_sq_ref,
    slab_ref,
    slab_sq_ref,
    new_rel_ref,
    new_rel_sq_ref,
    moved_ref,
    moved_sq_ref,
    land0,
    acc,
    land1,
    mid,
    land2,
    tot,
    part,
    gath,
    peer_half,
    grad,
    ss,
    rs,
):
    s, c = lax.axis_index("src"), lax.axis_index("dst")
    core, low, z = c % 2, (c // 2) % 2, c // 4
    g = s * 2 + low

    def in_plane(k):
        return (k // 2, (z * 2 + k % 2) * 2 + core)

    def along_z(k):
        return (s, (k * 2 + low) * 2 + core)

    peer = (s, c + 1 - 2 * core)
    right, left = (s, (c + 1) % 32), (s, (c + 31) % 32)

    def send(src, dst, n, device):
        copy = pltpu.make_async_remote_copy(
            src, dst, ss.at[n], rs.at[n], device_id=device, device_id_type=MESH
        )
        copy.start()
        return copy

    def wait_for(ref, sem):
        pltpu.make_async_copy(ref, ref, sem).wait()

    barrier = pltpu.get_barrier_semaphore()
    pl.semaphore_signal(barrier, inc=1, device_id=peer, device_id_type=MESH)
    pl.semaphore_signal(barrier, inc=1, device_id=left, device_id_type=MESH)
    for i in range(1, 16):
        pl.semaphore_signal(barrier, inc=1, device_id=in_plane((g + i) % 16), device_id_type=MESH)
    for i in range(1, 8):
        pl.semaphore_signal(barrier, inc=1, device_id=along_z((z + i) % 8), device_id_type=MESH)
    pl.semaphore_wait(barrier, 24)

    give = pl.ds(pl.multiple_of((1 - core) * HALF, 128), HALF)
    send(grad_ref.at[:, give], land0, 0, peer).wait()
    for k in range(100):
        rows, lane = slice(k // 4 * 8, k // 4 * 8 + 8), k % 4 * 128
        acc[k] = grad_ref[rows, pl.ds(pl.multiple_of(core * HALF + lane, 128), 128)] + land0[rows, lane : lane + 128]
    acc[100:112] = jnp.zeros((12, 8, 128), f32)
    for i in range(1, 16):
        k = (g + i) % 16
        send(acc.at[pl.ds(k * 7, 7)], land1.at[i - 1], 1, in_plane(k))
    hop = send(slab_ref, moved_ref, 6, right)
    hop_sq = send(slab_sq_ref, moved_sq_ref, 7, right)
    wait_for(land1, rs.at[1])
    mid[0:7] = acc[pl.ds(g * 7, 7)] + jnp.sum(land1[...], axis=0)
    mid[7:8] = jnp.zeros((1, 8, 128), f32)
    for i in range(1, 8):
        k = (z + i) % 8
        send(mid.at[k], land2.at[i - 1], 2, along_z(k))
    wait_for(land2, rs.at[2])
    tot[...] = mid[z] + jnp.sum(land2[...], axis=0)
    part[z] = tot[...]
    for i in range(1, 8):
        send(tot, part.at[z], 3, along_z((z + i) % 8))
    wait_for(land2, rs.at[3])
    for i in range(1, 16):
        send(part.at[pl.ds(0, 7)], gath.at[pl.ds(g * 7, 7)], 4, in_plane((g + i) % 16))
    gath[pl.ds(g * 7, 7)] = part[0:7]
    wait_for(land1, rs.at[4])
    swap = send(gath.at[pl.ds(0, 100)], peer_half, 5, peer)
    for k in range(100):
        rows, lane = slice(k // 4 * 8, k // 4 * 8 + 8), k % 4 * 128
        grad[rows, pl.ds(pl.multiple_of(core * HALF + lane, 128), 128)] = gath[k]
    swap.wait_recv()
    for k in range(100):
        rows, lane = slice(k // 4 * 8, k // 4 * 8 + 8), k % 4 * 128
        grad[rows, pl.ds(pl.multiple_of((1 - core) * HALF + lane, 128), 128)] = peer_half[k]
    new_rel_ref[...], new_rel_sq_ref[...] = adagrad(rel_ref[...], rel_sq_ref[...], grad[...])
    swap.wait_send()
    wait_for(land1, ss.at[1])
    wait_for(land2, ss.at[2])
    wait_for(land2, ss.at[3])
    wait_for(land1, ss.at[4])
    hop.wait()
    hop_sq.wait()


def exchange(rnd, grad, rel, rel_sq, slab, slab_sq):
    vmem = pl.BlockSpec(memory_space=pltpu.VMEM)

    def held(*shape):
        return pltpu.VMEM(shape, f32)

    return pl.pallas_call(
        exchange_kernel,
        out_shape=[
            jax.ShapeDtypeStruct((D, REL), f32),
            jax.ShapeDtypeStruct((1, REL), f32),
            jax.ShapeDtypeStruct((D, ROWS), f32),
            jax.ShapeDtypeStruct((1, ROWS), f32),
        ],
        in_specs=[vmem] * 5,
        out_specs=[vmem] * 4,
        scratch_shapes=[
            held(D, HALF),
            held(112, 8, 128),
            held(15, 7, 8, 128),
            held(8, 8, 128),
            held(7, 8, 128),
            held(8, 128),
            held(8, 8, 128),
            held(112, 8, 128),
            held(100, 8, 128),
            held(D, REL),
            pltpu.SemaphoreType.DMA((8,)),
            pltpu.SemaphoreType.DMA((8,)),
        ],
        compiler_params=pltpu.CompilerParams(
            collective_id=rnd, has_side_effects=True, vmem_limit_bytes=VMEM_LIMIT
        ),
        name=f"exchange{rnd}",
    )(grad, rel, rel_sq, slab, slab_sq)


def shards(
    src_rows,
    src_state,
    dst_rows,
    dst_state,
    relations,
    relation_state,
    block_tiles,
    src_offsets,
    dst_offsets,
    relation_ids,
    negative_ids,
):
    src, slab, rel = src_rows.T, dst_rows.T, relations.T
    src_sq, slab_sq, rel_sq = src_state[None, :], dst_state[None, :], relation_state[None, :]
    tiles = block_tiles.reshape(-1)
    neg_ids = jnp.pad(negative_ids, ((0, 0), (0, 0), (0, 64 - NEG)), constant_values=-1).reshape(
        ROUNDS, BLK // 2, 128
    )
    for rnd in range(ROUNDS):
        src, src_sq, slab, slab_sq, grad = run_round(
            rnd, tiles, src, src_sq, slab, slab_sq, rel, src_offsets, dst_offsets, relation_ids, neg_ids
        )
        rel, rel_sq, slab, slab_sq = exchange(rnd, grad, rel, rel_sq, slab, slab_sq)
    return src.T, slab.T, rel.T


def solution(mesh):
    own = ("src", "dst")
    ids = P(None, own, None)
    return jax.shard_map(
        shards,
        mesh=mesh,
        in_specs=(P(own, None), P(own), P(own, None), P(own), P(), P(), ids, ids, ids, ids, ids),
        out_specs=(P(own, None), P(own, None), P()),
        check_vma=False,
    )
```

time: 687 us -> 128 us (0.19); the launches traced: 676 us -> 128 us
  waiting for transfers between devices: 459 us -> 0 us
  Pallas kernels: 0 us -> 122 us
  local copies, waits for them, and re-layouts: 80.5 us -> 4.87 us
  matrix products: 58.8 us -> 0 us
  other arithmetic: 56.2 us -> 0 us
  between operations: 15.4 us -> 0.67 us
    psum x2 -> x0, waiting for transfers between devices: 459 us -> none  [shards(): rel_grad = lax.psum(rel_local, ('src', 'dst'))]
    pallas_call x0 -> x4, Pallas kernels: none -> 122 us  [the longest x2 81.7 us: exchange(): pl.pallas_call(exchange_kernel, out_shape=[jax.ShapeDtypeStruct((D, REL),...]
    dot_general x22 -> x0, matrix products: 58.8 us -> none  [the longest x2 9.04 us: local_terms(): jnp.einsum('ben,bnd->bed', neg_weight, neg_rows, precision=highest)]
    scatter-add x4 -> x0, other arithmetic: 39.2 us -> none  [the longest x2 26.1 us: local_terms(): rel_grad = jnp.zeros(rel_table.shape, jnp.float32).at[rel_ids.reshape(-1)...]
    gather x8 -> x0, local copies, waits for them, and re-layouts: 29.1 us -> none  [the longest x4 20.8 us: local_terms(): diagonal = jnp.take(rel_table, rel_ids, axis=0)]
    reshape x14 -> x2, local copies, waits for them, and re-layouts: 28.6 us -> 1.35 us  [the longest x1 0.69 us: shards(): tiles = block_tiles.reshape(-1)]
  transfers between devices with their start and end apart: 5 -> 0, of which waited for: 2 -> 0; matrix products, arithmetic and copies ran while one was open for 20% -> 0% of each run, Pallas kernels for 0% -> 0%
where the time goes in v1:
time: 128 us
  Pallas kernels  122 us (95%)
  local copies, waits for them, and re-layouts  4.87 us (4%)
    pallas_call x2, Pallas kernels, exchange(): pl.pallas_call(exchange_kernel, out_shape=[jax.ShapeDtypeStruct((D, REL),...  81.7 us
    pallas_call x2, Pallas kernels, run_round(): pl.pallas_call(functools.partial(round_kernel, rnd), out_shape=[jax.Shape...  40.6 us
    unnamed x9, local copies, waits for them, and re-layouts  3.52 us

profile of v1, /device:TPU:1, one launch (start us, length us, event | category | flops | bytes accessed | tf_op | source)
XLA Modules:
  0.0 127.8 jit_solution(18189124404337912601)
XLA Ops:
  0.6 0.0 copy-start.2
  0.6 0.7 copy-done.2
  1.3 0.0 copy-start.1
  1.3 0.1 copy.15
  1.4 0.7 reshape.12.tiles_ref
  2.1 0.0 copy-done.1
  2.1 0.7 reshape.13.neg_ids_ref
  2.8 20.3 %round0.1 = (f32[200,512]{1,0:T(8,128)}, f32[1,512]{1,0:T(1,128)}, f32[200,512]{1,0:T(8,128)}, f32[1,512]{1,0:T(1,128)}, f32[200,1024]{1,0:T(8,128)}) custom-call(s32[64]{0:T(128)} %reshape.12.tiles_ref, f32[200,512]{1,0:T(8,128)} %bitcast.12, f32[1,512]{1,0:T(1,128)} %bitcast.16, f32[200,512]{1,0:T(8,128)} %bitcast.13, f32[1,512]{1,0:T(1,128)} %bitcast.17, ...), custom_call_target="tpu_custom_call" | custom-call | tf_op jit(solution)/shard_map/round0/pallas_call | solution.py:166
  23.1 44.4 %exchange0.1 = (f32[200,1024]{1,0:T(8,128)}, f32[1,1024]{1,0:T(1,128)}, f32[200,512]{1,0:T(8,128)}, f32[1,512]{1,0:T(1,128)}) custom-call(f32[200,1024]{1,0:T(8,128)} %get-tuple-element.20.grad_ref, f32[200,1024]{1,0:T(8,128)} %bitcast.10, f32[1,1024]{1,0:T(1,128)} %bitcast.15, f32[200,512]{1,0:T(8,128)} %get-tuple-element.21.slab_ref, ...), custom_call_target="tpu_custom_call" | custom-call | tf_op jit(solution)/shard_map/exchange0/pallas_call | solution.py:298
  67.5 20.3 %round1.1 = (f32[200,512]{1,0:T(8,128)}, f32[1,512]{1,0:T(1,128)}, f32[200,512]{1,0:T(8,128)}, f32[1,512]{1,0:T(1,128)}, f32[200,1024]{1,0:T(8,128)}) custom-call(s32[64]{0:T(128)} %reshape.12.tiles_ref, f32[200,512]{1,0:T(8,128)} %get-tuple-element.18.src_ref, f32[1,512]{1,0:T(1,128)} %get-tuple-element.19.src_sq_ref, ...), custom_call_target="tpu_custom_call" | custom-call | tf_op jit(solution)/shard_map/round1/pallas_call | solution.py:166
  87.8 37.3 %exchange1.1 = (f32[200,1024]{1,0:T(8,128)}, f32[1,1024]{1,0:T(1,128)}, f32[200,512]{1,0:T(8,128)}, f32[1,512]{1,0:T(1,128)}) custom-call(f32[200,1024]{1,0:T(8,128)} %get-tuple-element.27.grad_ref, f32[200,1024]{1,0:T(8,128)} %get-tuple-element.25.rel_ref, f32[1,1024]{1,0:T(1,128)} %get-tuple-element.28.rel_sq_ref, f32[200,512]{1,0:T(8,128)} %get-tuple-element.29.slab_ref, ...), custom_call_target="tpu_custom_call" | custom-call | tf_op jit(solution)/shard_map/exchange1/pallas_call | solution.py:298
  125.1 0.0 copy-start
  125.1 1.9 %copy.18 = f32[512,200]{0,1:T(8,128)} copy(f32[512,200]{0,1:T(8,128)} %bitcast.14) | data formatting | bytes 819200
  127.0 0.0 copy-done
  127.0 0.9 copy.19
  (1 shorter events, 0.0 us)
Async XLA Ops:
  0.6 0.7 copy-start.2
  1.3 0.8 copy-start.1
  125.1 1.9 %copy-start = (f32[200,1024]{1,0:T(8,128)S(1)}, f32[200,1024]{1,0:T(8,128)}, u32[]{:S(2)}) copy-start(f32[200,1024]{1,0:T(8,128)} %get-tuple-element.32) | copy-start | bytes 2457604

commit v2 on v0

v2 whole, which is shorter than its diff:
```python
import jax
import jax.numpy as jnp
from jax import lax
from jax.experimental import pallas as pl
from jax.experimental.pallas import tpu as pltpu
from jax.sharding import PartitionSpec as P

MESH = pl.DeviceIdType.MESH
f32, bf16, i32 = jnp.float32, jnp.bfloat16, jnp.int32
learn_rate = 0.1
D, REL, TILE, NEG, ROWS, BLK, ROUNDS = 200, 1024, 128, 50, 512, 16, 2
EDGES = BLK * TILE
NEGS = BLK * 64
FEATS = D // 8
SHARE = 7
SHARES = 16 * SHARE
HALF_TILES = 4 * FEATS
VMEM_LIMIT = 60 << 20
NT = ((1,), (1,))
TN = ((0,), (0,))


def two_parts(value):
    high = value.astype(bf16)
    return high, (value - high.astype(f32)).astype(bf16)


def stacked(value):
    return jnp.concatenate(two_parts(value), axis=0)


def folded(value):
    half = value.shape[0] // 2
    return value[:half] + value[half:]


def dot(a, b, dims=((1,), (0,))):
    return lax.dot_general(a, b, (dims, ((), ())), preferred_element_type=f32)


def one_hot(ids, rows):
    places = lax.broadcasted_iota(i32, (rows, ids.shape[1]), 0)
    return jnp.where(places == ids, 1.0, 0.0).astype(bf16)


def adagrad(table, sums, grad):
    sums = sums + jnp.sum(grad * grad, axis=0, keepdims=True) * (1.0 / D)
    return table - grad * (learn_rate / jnp.sqrt(sums)), sums


def lanes_at(start, size):
    return pl.ds(start if isinstance(start, int) else pl.multiple_of(start, size), size)


def as_column(row):
    size = row.shape[1]
    square = lax.broadcasted_iota(i32, (size, size), 0) == lax.broadcasted_iota(i32, (size, size), 1)
    return jnp.sum(jnp.where(square, row.astype(f32), 0.0), axis=1, keepdims=True).astype(i32)


def place_ids(m):
    for rnd in range(ROUNDS):
        tiles = m.tiles[rnd]
        m.src_ids[rnd] = m.src_off[rnd] + as_column(tiles[0:1]) * TILE
        m.dst_ids[rnd] = m.dst_off[rnd] + as_column(tiles[1:2]) * TILE


def gather_negatives(rnd, m):
    ids = m.neg_ids[rnd]
    ids = jnp.concatenate([ids, jnp.full((BLK, 64 - NEG), -1, i32)], axis=1)
    for p in range(4):
        row = jnp.concatenate([ids[4 * p + j : 4 * p + j + 1, :] for j in range(4)], axis=1)
        hot = one_hot(row, ROWS)
        m.slab_hot[:, pl.ds(EDGES + p * 256, 256)] = hot
        negs = folded(dot(m.slab_parts[...], hot))
        here = pl.ds(p * 256, 256)
        m.neg_parts[:, here] = stacked(negs)
        for part, value in enumerate(two_parts(negs.T)):
            m.negs_turned[part, here, :] = value


def pair_ids(ref, rnd, p):
    return jnp.concatenate([ref[rnd, pl.ds(2 * p + j, 1), :] for j in range(2)], axis=1)


def gather_pair(rnd, m, p):
    both = lanes_at(p * 256, 256)
    src_hot = one_hot(pair_ids(m.src_ids, rnd, p), ROWS)
    dst_hot = one_hot(pair_ids(m.dst_ids, rnd, p), ROWS)
    m.src_hot[:, both] = src_hot
    m.slab_hot[:, both] = dst_hot
    m.heads[:, both] = folded(dot(m.src_parts[...], src_hot))
    m.tails[:, both] = folded(dot(m.slab_parts[...], dst_hot))
    m.rel_hot[:, both] = one_hot(pair_ids(m.rel_ids, rnd, p), REL)


def group_terms(m, first, count):
    pairs = range(count)
    both = [lanes_at((first + i) * 256, 256) for i in pairs]
    own = [lanes_at((first + i) * 128, 128) for i in pairs]
    lifted, parts, neg, score, weight = [], [], [], [], []
    for i in pairs:
        diagonal = folded(dot(m.rel_parts[...], m.rel_hot[:, both[i]]))
        m.diagonals[:, both[i]] = diagonal
        lifted.append(m.heads[:, both[i]] * diagonal)
        parts.append(two_parts(lifted[i]))
    for i in pairs:
        high, low = parts[i]
        turned = m.negs_turned[:, own[i], :]
        score.append(dot(turned.reshape(256, D), high))
        score[i] = folded(score[i]) + dot(turned[0], low)
    for i in pairs:
        pieces = [jax.nn.sigmoid(score[i][64 * j : 64 * j + 64, 128 * j : 128 * j + 128]) * (1.0 / NEG) for j in range(2)]
        nothing = jnp.zeros((64, 128), f32)
        weight.append(
            two_parts(
                jnp.concatenate(
                    [jnp.concatenate([pieces[0], nothing], axis=1), jnp.concatenate([nothing, pieces[1]], axis=1)], axis=0
                )
            )
        )
    for i in pairs:
        head, tail = m.heads[:, both[i]], m.tails[:, both[i]]
        negs = m.neg_parts[:, own[i]]
        positive = jnp.sum(lifted[i] * tail, axis=0, keepdims=True)
        pos_weight = -jax.nn.sigmoid(-positive)
        pulled = pos_weight * tail + folded(dot(negs, weight[i][0])) + dot(negs[:D], weight[i][1])
        m.src_terms[:, both[i]] = stacked(pulled * m.diagonals[:, both[i]])
        m.rel_terms[:, both[i]] = stacked(pulled * head)
        m.slab_terms[:, both[i]] = stacked(pos_weight * lifted[i])
    for i in pairs:
        neg_grad = folded(dot(jnp.concatenate(parts[i], axis=0), weight[i][0], NT)) + dot(parts[i][0], weight[i][1], NT)
        m.slab_terms[:, lanes_at(EDGES + (first + i) * 128, 128)] = stacked(neg_grad)


GROUP = 8


def all_terms(m):
    for i in range(BLK // 2 // GROUP):
        group_terms(m, i * GROUP, GROUP)


def gather_all(rnd, m):
    for p in range(BLK // 2):
        gather_pair(rnd, m, p)


def rel_gradient(m, out, half):
    for q in range(2):
        rows = lanes_at(half * (REL // 2) + q * 256, 256)
        grad = folded(dot(m.rel_terms[...], m.rel_hot[rows, :], NT))
        for j in range(2):
            piece = grad[:, j * 128 : j * 128 + 128]
            out[half, pl.ds((2 * q + j) * FEATS, FEATS)] = piece.reshape(FEATS, 8, 128)


def row_update(terms, hot, table, sums, new_table, new_sums, q):
    rows = pl.ds(q * 256, 256)
    grad = folded(dot(terms[...], hot[rows, :], NT))
    new_table[:, rows], new_sums[:, rows] = adagrad(table[:, rows], sums[:, rows], grad)


def rel_update(m, half, table, sums, grad, new_table, new_sums):
    for j in range(4):
        rows = lanes_at(half * (REL // 2) + j * 128, 128)
        piece = grad[half, pl.ds(j * FEATS, FEATS)].reshape(D, 128)
        new, new_sq = adagrad(table[:, rows], sums[:, rows], piece)
        new_table[:, rows] = new
        if new_sums is not None:
            new_sums[:, rows] = new_sq
            m.rel_parts[:, rows] = stacked(new)


PLANE = sorted(
    ((dx, dy) for dx in range(4) for dy in range(4) if dx or dy),
    key=lambda step: -min(step[0], 4 - step[0]) - min(step[1], 4 - step[1]),
)


class Refs:
    def __init__(self, names, refs):
        for name, ref in zip(names, refs, strict=True):
            setattr(self, name, ref)


INPUTS = (
    ("tiles", "src0", "src_sq0", "slab0", "slab_sq0", "rel0", "rel_sq0")
    + ("src_off", "dst_off", "rel_ids", "neg_ids")
)
OUTPUTS = ("src2", "slab_out", "rel2")
SCRATCH = {
    "src_ids": ((ROUNDS, BLK, TILE), i32),
    "dst_ids": ((ROUNDS, BLK, TILE), i32),
    "src_parts": ((2 * D, ROWS), bf16),
    "slab_parts": ((2 * D, ROWS), bf16),
    "rel_parts": ((2 * D, REL), bf16),
    "rel_hot": ((REL, EDGES), bf16),
    "src_hot": ((ROWS, EDGES), bf16),
    "slab_hot": ((ROWS, EDGES + NEGS), bf16),
    "neg_parts": ((2 * D, NEGS), bf16),
    "negs_turned": ((2, NEGS, D), bf16),
    "diagonals": ((D, EDGES), f32),
    "heads": ((D, EDGES), f32),
    "tails": ((D, EDGES), f32),
    "src_terms": ((2 * D, EDGES), bf16),
    "slab_terms": ((2 * D, EDGES + NEGS), bf16),
    "rel_terms": ((2 * D, EDGES), bf16),
    "src1": ((D, ROWS), f32),
    "src_sq1": ((1, ROWS), f32),
    "src_sq2": ((1, ROWS), f32),
    "rel1": ((D, REL), f32),
    "rel_sq1": ((1, REL), f32),
    "slab_new": ((2, D, ROWS), f32),
    "slab_sq_new": ((2, 1, ROWS), f32),
    "slab1": ((D, ROWS), f32),
    "slab_sq1": ((1, ROWS), f32),
    "mine": ((2, 2, SHARES, 8, 128), f32),
    "land0": ((2, HALF_TILES, 8, 128), f32),
    "land1": ((2, 15, SHARE, 8, 128), f32),
    "mid": ((2, SHARE, 8, 128), f32),
    "land2": ((2, 7, SHARE, 8, 128), f32),
    "total": ((2, 2, SHARES, 8, 128), f32),
}


def kernel(*refs):
    m = Refs((*INPUTS, *OUTPUTS, *SCRATCH, "ss", "rs"), refs)
    s, c = lax.axis_index("src"), lax.axis_index("dst")
    core, low, z = c % 2, (c // 2) % 2, c // 4
    g = s * 2 + low
    x, y = s // 4 * 2 + low, s % 4

    def plane_index(x, y):
        return (x // 2 * 4 + y) * 2 + x % 2

    def in_plane(k):
        return (k // 2, (z * 2 + k % 2) * 2 + core)

    def along_z(k):
        return (s, (k * 2 + low) * 2 + core)

    peer = (s, c + 1 - 2 * core)
    right, left = (s, (c + 1) % 32), (s, (c + 31) % 32)

    def wait_for(ref, sem):
        pltpu.make_async_copy(ref, ref, sem).wait()

    barrier = pltpu.get_barrier_semaphore()
    for device in (
        [peer, left]
        + [in_plane((g + i) % 16) for i in range(1, 16)]
        + [along_z((z + i) % 8) for i in range(1, 8)]
    ):
        pl.semaphore_signal(barrier, inc=1, device_id=device, device_id_type=MESH)

    place_ids(m)
    m.slab_parts[...] = stacked(m.slab0[...])
    m.src_parts[...] = stacked(m.src0[...])
    m.rel_parts[...] = stacked(m.rel0[...])
    gather_negatives(0, m)
    gather_all(0, m)

    for rnd in range(ROUNDS):
        ss, rs = m.ss.at[rnd], m.rs.at[rnd]
        mine, total = m.mine.at[rnd], m.total.at[rnd]
        land0, land1, land2, mid = m.land0.at[rnd], m.land1.at[rnd], m.land2.at[rnd], m.mid.at[rnd]
        if rnd == 0:
            src, src_sq, slab, slab_sq, rel, rel_sq = m.src0, m.src_sq0, m.slab0, m.slab_sq0, m.rel0, m.rel_sq0
            new_src, new_src_sq, new_rel, new_rel_sq = m.src1, m.src_sq1, m.rel1, m.rel_sq1
        else:
            src, src_sq, slab, slab_sq, rel, rel_sq = m.src1, m.src_sq1, m.slab1, m.slab_sq1, m.rel1, m.rel_sq1
            new_src, new_src_sq, new_rel, new_rel_sq = m.src2, m.src_sq2, m.rel2, None

        def send(what, where, n, device):
            copy = pltpu.make_async_remote_copy(
                what, where, ss.at[n], rs.at[n], device_id=device, device_id_type=MESH
            )
            copy.start()
            return copy

        all_terms(m)
        rel_gradient(m, mine, 1 - core)

        if rnd == 0:
            pl.semaphore_wait(barrier, 24)
        swap = send(mine.at[1 - core, pl.ds(0, HALF_TILES)], land0, 0, peer)
        rel_gradient(m, mine, core)
        mine[core, HALF_TILES:SHARES] = jnp.zeros((SHARES - HALF_TILES, 8, 128), f32)
        swap.wait_recv()
        mine[core, 0:HALF_TILES] += land0[...]
        for i, (dx, dy) in enumerate(PLANE):
            k = plane_index((x + dx) % 4, (y + dy) % 4)
            send(mine.at[core, pl.ds(k * SHARE, SHARE)], land1.at[i], 1, in_plane(k))
        for q in range(2):
            row_update(m.slab_terms, m.slab_hot, slab, slab_sq, m.slab_new.at[rnd], m.slab_sq_new.at[rnd], q)
        hop = send(m.slab_new.at[rnd], m.slab1 if rnd == 0 else m.slab_out, 2, right)
        if rnd == 0:
            hop_sq = send(m.slab_sq_new.at[rnd], m.slab_sq1, 3, right)
        wait_for(land1, rs.at[1])
        mid[...] = mine[core, pl.ds(g * SHARE, SHARE)] + jnp.sum(land1[...], axis=0)
        for i in (4, 3, 5, 2, 6, 1, 7):
            send(mid, land2.at[i - 1], 4, along_z((z + i) % 8))
        for q in range(2):
            row_update(m.src_terms, m.src_hot, src, src_sq, new_src, new_src_sq, q)
        wait_for(land2, rs.at[4])
        part = total.at[core, pl.ds(g * SHARE, SHARE)]
        part[...] = mid[...] + jnp.sum(land2[...], axis=0)
        for dx, dy in PLANE:
            send(part, part, 5, in_plane(plane_index((x + dx) % 4, (y + dy) % 4)))
        if rnd == 0:
            hop.wait_recv()
            hop_sq.wait_recv()
            m.slab_parts[...] = stacked(m.slab1[...])
            m.src_parts[...] = stacked(m.src1[...])
            gather_negatives(1, m)
            gather_all(1, m)
        wait_for(land1, rs.at[5])
        half = total.at[core, pl.ds(0, HALF_TILES)]
        back = send(half, half, 6, peer)
        rel_update(m, core, rel, rel_sq, total, new_rel, new_rel_sq)
        back.wait_recv()
        rel_update(m, 1 - core, rel, rel_sq, total, new_rel, new_rel_sq)
        if rnd == 1:
            hop.wait_recv()
        swap.wait_send()
        wait_for(land1, ss.at[1])
        hop.wait_send()
        if rnd == 0:
            hop_sq.wait_send()
        wait_for(land2, ss.at[4])
        wait_for(land1, ss.at[5])
        back.wait_send()


def both_rounds(*args):
    vmem = pl.BlockSpec(memory_space=pltpu.VMEM)
    return pl.pallas_call(
        kernel,
        out_shape=[
            jax.ShapeDtypeStruct((D, ROWS), f32),
            jax.ShapeDtypeStruct((D, ROWS), f32),
            jax.ShapeDtypeStruct((D, REL), f32),
        ],
        in_specs=[vmem] * 11,
        out_specs=[vmem] * 3,
        scratch_shapes=[pltpu.VMEM(*of) for of in SCRATCH.values()]
        + [pltpu.SemaphoreType.DMA((2, 7)), pltpu.SemaphoreType.DMA((2, 7))],
        compiler_params=pltpu.CompilerParams(
            collective_id=0, has_side_effects=True, vmem_limit_bytes=VMEM_LIMIT
        ),
        name="both_rounds",
    )(*args)


def shards(
    src_rows,
    src_state,
    dst_rows,
    dst_state,
    relations,
    relation_state,
    block_tiles,
    src_offsets,
    dst_offsets,
    relation_ids,
    negative_ids,
):
    src, slab, rel = both_rounds(
        block_tiles.transpose(0, 2, 1),
        src_rows.T,
        src_state[None, :],
        dst_rows.T,
        dst_state[None, :],
        relations.T,
        relation_state[None, :],
        src_offsets,
        dst_offsets,
        relation_ids,
        negative_ids,
    )
    return src.T, slab.T, rel.T


def solution(mesh):
    own = ("src", "dst")
    ids = P(None, own, None)
    return jax.shard_map(
        shards,
        mesh=mesh,
        in_specs=(P(own, None), P(own), P(own, None), P(own), P(), P(), ids, ids, ids, ids, ids),
        out_specs=(P(own, None), P(own, None), P()),
        check_vma=False,
    )
```

time: 687 us -> 87 us (0.13); the launches traced: 676 us -> 86.9 us
  waiting for transfers between devices: 459 us -> 0 us
  Pallas kernels: 0 us -> 82.7 us
  local copies, waits for them, and re-layouts: 80.5 us -> 3.53 us
  matrix products: 58.8 us -> 0 us
  other arithmetic: 56.2 us -> 0 us
  between operations: 15.4 us -> 0.66 us
    psum x2 -> x0, waiting for transfers between devices: 459 us -> none  [shards(): rel_grad = lax.psum(rel_local, ('src', 'dst'))]
    pallas_call x0 -> x1, Pallas kernels: none -> 82.7 us  [both_rounds(): pl.pallas_call(kernel, out_shape=[jax.ShapeDtypeStruct((D, ROWS), f32), j...]
    dot_general x22 -> x0, matrix products: 58.8 us -> none  [the longest x2 9.04 us: local_terms(): jnp.einsum('ben,bnd->bed', neg_weight, neg_rows, precision=highest)]
    scatter-add x4 -> x0, other arithmetic: 39.2 us -> none  [the longest x2 26.1 us: local_terms(): rel_grad = jnp.zeros(rel_table.shape, jnp.float32).at[rel_ids.reshape(-1)...]
    gather x8 -> x0, local copies, waits for them, and re-layouts: 29.1 us -> none  [the longest x4 20.8 us: local_terms(): diagonal = jnp.take(rel_table, rel_ids, axis=0)]
    reshape x14 -> x0, local copies, waits for them, and re-layouts: 28.6 us -> none  [the longest x4 14.6 us: store_tiles(): flattened = pieces.reshape(block_count, tile_rows * features)]
  transfers between devices with their start and end apart: 5 -> 0, of which waited for: 2 -> 0; matrix products, arithmetic and copies ran while one was open for 20% -> 0% of each run, Pallas kernels for 0% -> 0%
where the time goes in v2:
time: 87 us; the launch traced here: 86.9 us
  Pallas kernels  82.7 us (95%)
  local copies, waits for them, and re-layouts  3.53 us (4%)
    pallas_call x1, Pallas kernels, both_rounds(): pl.pallas_call(kernel, out_shape=[jax.ShapeDtypeStruct((D, ROWS), f32), j...  82.7 us
    unnamed x7, local copies, waits for them, and re-layouts  3.53 us

profile of v2, /device:TPU:1, one launch (start us, length us, event | category | flops | bytes accessed | tf_op | source)
XLA Modules:
  0.0 86.9 jit_solution(11148374174054860046)
XLA Ops:
  0.6 82.7 %both_rounds.1 = (f32[200,512]{1,0:T(8,128)}, f32[200,512]{1,0:T(8,128)}, f32[200,1024]{1,0:T(8,128)}) custom-call(s32[2,2,16]{2,1,0:T(2,128)} %bitcast.17, f32[200,512]{1,0:T(8,128)} %bitcast.14, f32[1,512]{1,0:T(1,128)} %bitcast.18, f32[200,512]{1,0:T(8,128)} %bitcast.15, f32[1,512]{1,0:T(1,128)} %bitcast.19, f32[200,1024]{1,0:T(8,128)} %bitcast.11, ...), custom_call_target="tpu_custom_call" | custom-call | tf_op jit(solution)/shard_map/both_rounds/pallas_call | solution.py:338
  83.3 0.0 copy-start.1
  83.3 0.0 copy-start
  83.4 1.9 %copy.17 = f32[512,200]{0,1:T(8,128)} copy(f32[512,200]{0,1:T(8,128)} %bitcast.13) | data formatting | bytes 819200
  85.2 0.0 copy-done.1
  85.2 0.8 copy.18
  86.0 0.0 copy-done
  86.0 0.9 %copy.19 = f32[1024,200]{0,1:T(8,128)} copy(f32[1024,200]{0,1:T(8,128)S(1)} %bitcast.10) | data formatting | bytes 1638400
Async XLA Ops:
  83.3 1.9 %copy-start.1 = (f32[200,512]{1,0:T(8,128)S(1)}, f32[200,512]{1,0:T(8,128)}, u32[]{:S(2)}) copy-start(f32[200,512]{1,0:T(8,128)} %get-tuple-element.7) | copy-start | bytes 1228804
  83.3 2.6 %copy-start = (f32[200,1024]{1,0:T(8,128)S(1)}, f32[200,1024]{1,0:T(8,128)}, u32[]{:S(2)}) copy-start(f32[200,1024]{1,0:T(8,128)} %get-tuple-element.8) | copy-start | bytes 2457604

commit v3 on v2

--- a/solution.py
+++ b/solution.py
@@ -12,9 +12,10 @@
 EDGES = BLK * TILE
 NEGS = BLK * 64
 FEATS = D // 8
-SHARE = 7
-SHARES = 16 * SHARE
 HALF_TILES = 4 * FEATS
+PLANE_SHARE, LINE_SHARE = 5, 3
+PLANE_TILES = 16 * PLANE_SHARE
+TILES = PLANE_TILES + 8 * LINE_SHARE
 VMEM_LIMIT = 60 << 20
 NT = ((1,), (1,))
 TN = ((0,), (0,))
@@ -177,6 +178,12 @@
     key=lambda step: -min(step[0], 4 - step[0]) - min(step[1], 4 - step[1]),
 )
 
+LINE = (4, 3, 5, 2, 6, 1, 7)
+STEPS = [
+    (to_plane, i)
+    for _, to_plane, i in sorted([(i / 7, False, i) for i in range(7)] + [(i / 15, True, i) for i in range(15)])
+]
+
 
 class Refs:
     def __init__(self, names, refs):
@@ -215,12 +222,15 @@
     "slab_sq_new": ((2, 1, ROWS), f32),
     "slab1": ((D, ROWS), f32),
     "slab_sq1": ((1, ROWS), f32),
-    "mine": ((2, 2, SHARES, 8, 128), f32),
+    "mine": ((2, 2, TILES, 8, 128), f32),
     "land0": ((2, HALF_TILES, 8, 128), f32),
-    "land1": ((2, 15, SHARE, 8, 128), f32),
-    "mid": ((2, SHARE, 8, 128), f32),
-    "land2": ((2, 7, SHARE, 8, 128), f32),
-    "total": ((2, 2, SHARES, 8, 128), f32),
+    "plane_in": ((2, 15, PLANE_SHARE, 8, 128), f32),
+    "line_in": ((2, 7, LINE_SHARE, 8, 128), f32),
+    "plane_mid": ((2, PLANE_SHARE, 8, 128), f32),
+    "line_mid": ((2, LINE_SHARE, 8, 128), f32),
+    "plane_in2": ((2, 7, PLANE_SHARE, 8, 128), f32),
+    "line_in2": ((2, 15, LINE_SHARE, 8, 128), f32),
+    "total": ((2, 2, TILES, 8, 128), f32),
 }
 
 
@@ -242,6 +252,12 @@
 
     peer = (s, c + 1 - 2 * core)
     right, left = (s, (c + 1) % 32), (s, (c + 31) % 32)
+
+    def plane_of(i):
+        return plane_index((x + PLANE[i][0]) % 4, (y + PLANE[i][1]) % 4)
+
+    def line_of(i):
+        return (z + LINE[i]) % 8
 
     def wait_for(ref, sem):
         pltpu.make_async_copy(ref, ref, sem).wait()
@@ -264,7 +280,9 @@
     for rnd in range(ROUNDS):
         ss, rs = m.ss.at[rnd], m.rs.at[rnd]
         mine, total = m.mine.at[rnd], m.total.at[rnd]
-        land0, land1, land2, mid = m.land0.at[rnd], m.land1.at[rnd], m.land2.at[rnd], m.mid.at[rnd]
+        land0 = m.land0.at[rnd]
+        plane_in, plane_mid, plane_in2 = m.plane_in.at[rnd], m.plane_mid.at[rnd], m.plane_in2.at[rnd]
+        line_in, line_mid, line_in2 = m.line_in.at[rnd], m.line_mid.at[rnd], m.line_in2.at[rnd]
         if rnd == 0:
             src, src_sq, slab, slab_sq, rel, rel_sq = m.src0, m.src_sq0, m.slab0, m.slab_sq0, m.rel0, m.rel_sq0
             new_src, new_src_sq, new_rel, new_rel_sq = m.src1, m.src_sq1, m.rel1, m.rel_sq1
@@ -286,28 +304,59 @@
             pl.semaphore_wait(barrier, 24)
         swap = send(mine.at[1 - core, pl.ds(0, HALF_TILES)], land0, 0, peer)
         rel_gradient(m, mine, core)
-        mine[core, HALF_TILES:SHARES] = jnp.zeros((SHARES - HALF_TILES, 8, 128), f32)
+        mine[core, HALF_TILES:TILES] = jnp.zeros((TILES - HALF_TILES, 8, 128), f32)
         swap.wait_recv()
         mine[core, 0:HALF_TILES] += land0[...]
-        for i, (dx, dy) in enumerate(PLANE):
-            k = plane_index((x + dx) % 4, (y + dy) % 4)
-            send(mine.at[core, pl.ds(k * SHARE, SHARE)], land1.at[i], 1, in_plane(k))
+        for to_plane, i in STEPS:
+            if to_plane:
+                k = plane_of(i)
+                send(mine.at[core, pl.ds(k * PLANE_SHARE, PLANE_SHARE)], plane_in.at[i], 1, in_plane(k))
+            else:
+                k = line_of(i)
+                send(mine.at[core, pl.ds(PLANE_TILES + k * LINE_SHARE, LINE_SHARE)], line_in.at[i], 7, along_z(k))
         for q in range(2):
             row_update(m.slab_terms, m.slab_hot, slab, slab_sq, m.slab_new.at[rnd], m.slab_sq_new.at[rnd], q)
-        hop = send(m.slab_new.at[rnd], m.slab1 if rnd == 0 else m.slab_out, 2, right)
+        hop = pltpu.make_async_remote_copy(
+            m.slab_new.at[rnd],
+            m.slab1 if rnd == 0 else m.slab_out,
+            ss.at[2],
+            rs.at[2],
+            device_id=right,
+            device_id_type=MESH,
+        )
+
+        @pl.when(core == 0)
+        def _():
+            hop.start()
+
         if rnd == 0:
             hop_sq = send(m.slab_sq_new.at[rnd], m.slab_sq1, 3, right)
-        wait_for(land1, rs.at[1])
-        mid[...] = mine[core, pl.ds(g * SHARE, SHARE)] + jnp.sum(land1[...], axis=0)
-        for i in (4, 3, 5, 2, 6, 1, 7):
-            send(mid, land2.at[i - 1], 4, along_z((z + i) % 8))
+        own_plane = pl.ds(g * PLANE_SHARE, PLANE_SHARE)
+        own_line = pl.ds(PLANE_TILES + z * LINE_SHARE, LINE_SHARE)
+        wait_for(line_in, rs.at[7])
+        line_mid[...] = mine[core, own_line] + jnp.sum(line_in[...], axis=0)
+        for i in range(15):
+            send(line_mid, line_in2.at[i], 8, in_plane(plane_of(i)))
+        wait_for(plane_in, rs.at[1])
+        plane_mid[...] = mine[core, own_plane] + jnp.sum(plane_in[...], axis=0)
+        for i in range(7):
+            send(plane_mid, plane_in2.at[i], 4, along_z(line_of(i)))
+
+        @pl.when(core == 1)
+        def _():
+            hop.start()
+
         for q in range(2):
             row_update(m.src_terms, m.src_hot, src, src_sq, new_src, new_src_sq, q)
-        wait_for(land2, rs.at[4])
-        part = total.at[core, pl.ds(g * SHARE, SHARE)]
-        part[...] = mid[...] + jnp.sum(land2[...], axis=0)
-        for dx, dy in PLANE:
-            send(part, part, 5, in_plane(plane_index((x + dx) % 4, (y + dy) % 4)))
+        plane_part, line_part = total.at[core, own_plane], total.at[core, own_line]
+        wait_for(line_in2, rs.at[8])
+        line_part[...] = line_mid[...] + jnp.sum(line_in2[...], axis=0)
+        for i in range(7):
+            send(line_part, line_part, 9, along_z(line_of(i)))
+        wait_for(plane_in2, rs.at[4])
+        plane_part[...] = plane_mid[...] + jnp.sum(plane_in2[...], axis=0)
+        for i in range(15):
+            send(plane_part, plane_part, 5, in_plane(plane_of(i)))
         if rnd == 0:
             hop.wait_recv()
             hop_sq.wait_recv()
@@ -315,7 +364,8 @@
             m.src_parts[...] = stacked(m.src1[...])
             gather_negatives(1, m)
             gather_all(1, m)
-        wait_for(land1, rs.at[5])
+        wait_for(line_in, rs.at[9])
+        wait_for(plane_in, rs.at[5])
         half = total.at[core, pl.ds(0, HALF_TILES)]
         back = send(half, half, 6, peer)
         rel_update(m, core, rel, rel_sq, total, new_rel, new_rel_sq)
@@ -324,12 +374,15 @@
         if rnd == 1:
             hop.wait_recv()
         swap.wait_send()
-        wait_for(land1, ss.at[1])
+        wait_for(plane_in, ss.at[1])
+        wait_for(line_in, ss.at[7])
         hop.wait_send()
         if rnd == 0:
             hop_sq.wait_send()
-        wait_for(land2, ss.at[4])
-        wait_for(land1, ss.at[5])
+        wait_for(plane_in2, ss.at[4])
+        wait_for(line_in2, ss.at[8])
+        wait_for(plane_in, ss.at[5])
+        wait_for(line_in, ss.at[9])
         back.wait_send()
 
 
@@ -338,19 +391,41 @@
     return pl.pallas_call(
         kernel,
         out_shape=[
-            jax.ShapeDtypeStruct((D, ROWS), f32),
-            jax.ShapeDtypeStruct((D, ROWS), f32),
-            jax.ShapeDtypeStruct((D, REL), f32),
+            pltpu.VMEM((D, ROWS), f32),
+            pltpu.VMEM((D, ROWS), f32),
+            pltpu.VMEM((D, REL), f32),
         ],
         in_specs=[vmem] * 11,
         out_specs=[vmem] * 3,
         scratch_shapes=[pltpu.VMEM(*of) for of in SCRATCH.values()]
-        + [pltpu.SemaphoreType.DMA((2, 7)), pltpu.SemaphoreType.DMA((2, 7))],
+        + [pltpu.SemaphoreType.DMA((2, 10)), pltpu.SemaphoreType.DMA((2, 10))],
         compiler_params=pltpu.CompilerParams(
             collective_id=0, has_side_effects=True, vmem_limit_bytes=VMEM_LIMIT
         ),
         name="both_rounds",
     )(*args)
+
+
+def settle_kernel(*refs):
+    copies = [pltpu.make_async_copy(refs[i], refs[3 + i], refs[6].at[i]) for i in range(3)]
+    for copy in copies:
+        copy.start()
+    for copy in copies:
+        copy.wait()
+
+
+def settle(*arrays):
+    arrays = [pltpu.with_memory_space_constraint(a, pltpu.VMEM) for a in arrays]
+    anywhere = pl.BlockSpec(memory_space=pl.ANY)
+    return pl.pallas_call(
+        settle_kernel,
+        out_shape=[jax.ShapeDtypeStruct(a.shape, a.dtype) for a in arrays],
+        in_specs=[pl.BlockSpec(memory_space=pltpu.VMEM)] * 3,
+        out_specs=[anywhere] * 3,
+        scratch_shapes=[pltpu.SemaphoreType.DMA((3,))],
+        compiler_params=pltpu.CompilerParams(vmem_limit_bytes=8 << 20),
+        name="settle",
+    )(*arrays)
 
 
 def shards(
@@ -366,7 +441,7 @@
     relation_ids,
     negative_ids,
 ):
-    src, slab, rel = both_rounds(
+    results = both_rounds(
         block_tiles.transpose(0, 2, 1),
         src_rows.T,
         src_state[None, :],
@@ -379,6 +454,7 @@
         relation_ids,
         negative_ids,
     )
+    src, slab, rel = settle(*results)
     return src.T, slab.T, rel.T
 
 

time: 87 us -> 74.1 us (0.85)
  Pallas kernels: 82.7 us -> 73.2 us
  local copies, waits for them, and re-layouts: 3.53 us -> 0 us
    pallas_call x1 -> x2, Pallas kernels: 82.7 us -> 73.2 us  [the longest x1 72 us: both_rounds(): pl.pallas_call(kernel, out_shape=[pltpu.VMEM((D, ROWS), f32), pltpu.VMEM(...]
    unnamed x7 -> x0, local copies, waits for them, and re-layouts: 3.53 us -> none
where the time goes in v3:
time: 74.1 us; the launch traced here: 74 us
  Pallas kernels  73.2 us (99%)
  between operations  0.8 us (1%)
    pallas_call x1, Pallas kernels, both_rounds(): pl.pallas_call(kernel, out_shape=[pltpu.VMEM((D, ROWS), f32), pltpu.VMEM(...  72 us

profile of v3, /device:TPU:1, one launch (start us, length us, event | category | flops | bytes accessed | tf_op | source)
XLA Modules:
  0.0 74.0 jit_solution(7322249325175599418)
XLA Ops:
  0.6 72.0 %both_rounds.1 = (f32[200,512]{1,0:T(8,128)S(1)}, f32[200,512]{1,0:T(8,128)S(1)}, f32[200,1024]{1,0:T(8,128)S(1)}) custom-call(s32[2,2,16]{2,1,0:T(2,128)} %bitcast.14, f32[200,512]{1,0:T(8,128)} %bitcast.11, f32[1,512]{1,0:T(1,128)} %bitcast.15, f32[200,512]{1,0:T(8,128)} %bitcast.12, f32[1,512]{1,0:T(1,128)} %bitcast.16, f32[200,1024]{1,0:T(8,128)} %bitcast.10, ...), custom_call_target="tpu_custom_call" | custom-call | tf_op jit(solution)/shard_map/both_rounds/pallas_call | solution.py:391
  72.6 1.2 %settle.1 = (f32[200,512]{1,0:T(8,128)}, f32[200,512]{1,0:T(8,128)}, f32[200,1024]{1,0:T(8,128)}) custom-call(f32[200,512]{1,0:T(8,128)S(1)} %get-tuple-element.9.refs_0_, f32[200,512]{1,0:T(8,128)S(1)} %get-tuple-element.10.refs_1_, f32[200,1024]{1,0:T(8,128)S(1)} %get-tuple-element.11.refs_2_), custom_call_target="tpu_custom_call" | custom-call | tf_op jit(solution)/shard_map/settle/pallas_call | solution.py:420
